TPU v7x, 256 devices: a whole 4x4x8 slice. The times are simulated.
256 devices in a mesh: ctx: 128 (over x_hi, z, y, core), tp: 2 (over x_lo).
Axes of the slice: x: 4 (x_hi: 2, x_lo: 2; x = x_hi * 2 + x_lo), y: 4, z: 8, core: 2. Of those that a mesh axis runs over, the one named last changes fastest.
Arguments:
- query: bfloat16 [32768, 2048], P('ctx', 'tp'), may hold values from -6 to 6
- key_in: bfloat16 [32768, 2048], P('ctx', 'tp'), may hold values from -6 to 6
- value: bfloat16 [32768, 2048], P('ctx', 'tp'), may hold values from -6 to 6
- grad_out: bfloat16 [32768, 2048], P('ctx', 'tp'), may hold values from -6 to 6
- residue: float32 [16, 2048], P(None, 'tp'), may hold values from -0.125 to 0.125
- rate: float32 [16, 2048], P(None, 'tp'), may hold values from 0.5 to 1024
Outputs:
- grad_query: bfloat16 [32768, 2048], P('ctx', 'tp')
- grad_key: bfloat16 [32768, 2048], P('ctx', 'tp')
- grad_value: bfloat16 [32768, 2048], P('ctx', 'tp')
- grad_residue: float32 [16, 2048], P(None, 'tp')
- grad_rate: float32 [16, 2048], P(None, 'tp')
All inputs are finite; a program needn't handle non-finite values.
Results may differ from a plain program's by a relative error of at most 0.0058.
Values may be sent and summed in bfloat16 or wider, within the bound.
A program may use at most 320 MiB of HBM per device.

v0:
```python
from functools import partial
import jax
import jax.numpy as jnp
from jax import lax
from jax.sharding import PartitionSpec as P

BLK = 128
HIGH = lax.Precision.HIGHEST


def combine_fwd(lam, earlier, later):
    span_a, state_a, moment_a = earlier
    span_b, state_b, moment_b = later
    decay = jnp.exp(-lam * span_b)
    return (
        span_a + span_b,
        decay * state_a + state_b,
        decay * (moment_a + span_b * state_a) + moment_b,
    )


def combine_rev(lam, earlier, later):
    span_a, state_a = earlier
    span_b, state_b = later
    return (span_a + span_b, jnp.exp(-lam * span_b) * state_a + state_b)


def layouts():
    return ("cbj", "cbi", "cmb", 2)


def prepare(gated, grad_conv, rate, seq_len):
    lay_j, lay_i, lay_s, axis_b = layouts()
    lam = rate / seq_len
    pos = jnp.arange(BLK, dtype=jnp.float32)[:, None, None]
    head = jnp.exp(-lam * pos)
    head_next = jnp.exp(-lam * (pos + 1.0))
    tail = jnp.exp(-lam * (BLK - 1.0 - pos))
    back = jnp.exp(-lam * (BLK - pos))
    chans, rows = gated.shape
    blocks = rows // BLK
    gated_b = gated.astype(jnp.float32).reshape(chans, blocks, BLK)
    grad_b = grad_conv.astype(jnp.float32).reshape(chans, blocks, BLK)
    lam_s = lam.T[:, :, None]
    spans = jnp.full((1, 1, blocks), float(BLK), jnp.float32)
    state_sum = jnp.einsum(lay_j + ",jmc->" + lay_s, gated_b, tail, precision=HIGH)
    moment_sum = jnp.einsum(
        lay_j + ",jmc->" + lay_s, gated_b, (BLK - 1.0 - pos) * tail, precision=HIGH
    )
    back_sum = jnp.einsum(lay_i + ",imc->" + lay_s, grad_b, head, precision=HIGH)
    fwd_incl = lax.associative_scan(
        partial(combine_fwd, lam_s), (spans, state_sum, moment_sum), axis=axis_b
    )
    rev_incl = lax.associative_scan(
        partial(combine_rev, lam_s), (spans, back_sum), reverse=True, axis=axis_b
    )
    tables = (lam_s, pos, head, head_next, back)
    return (tables, gated_b, grad_b, fwd_incl, rev_incl)


def shift_down(arr, axis_b):
    count = arr.shape[axis_b]
    first = jnp.zeros_like(lax.slice_in_dim(arr, 0, 1, axis=axis_b))
    return jnp.concatenate([first, lax.slice_in_dim(arr, 0, count - 1, axis=axis_b)], axis_b)


def shift_up(arr, axis_b):
    count = arr.shape[axis_b]
    last = jnp.zeros_like(lax.slice_in_dim(arr, 0, 1, axis=axis_b))
    return jnp.concatenate([lax.slice_in_dim(arr, 1, count, axis=axis_b), last], axis_b)


def finish(tables, gated_b, grad_b, fwd_incl, rev_incl, fwd_in, rev_in, residue, seq_len):
    lam_s, pos, head, head_next, back = tables
    lay_j, lay_i, lay_s, axis_b = layouts()
    fwd_excl = tuple((shift_down(part, axis_b) for part in fwd_incl))
    rev_excl = tuple((shift_up(part, axis_b) for part in rev_incl))
    _, state_in, moment_in = combine_fwd(lam_s, fwd_in, fwd_excl)
    _, back_in = combine_rev(lam_s, rev_in, rev_excl)
    lag = jnp.arange(BLK)
    onehot = (lag[:, None, None] - lag[None, :, None] == lag[None, None, :]).astype(jnp.float32)
    short_filter = jnp.einsum("mc,kmc->kc", residue, head, precision=HIGH)
    toeplitz = jnp.einsum("kc,ijk->cij", short_filter, onehot, precision=HIGH)
    conv = jnp.einsum("cij," + lay_j + "->" + lay_i, toeplitz, gated_b, precision=HIGH)
    conv = conv + jnp.einsum(
        "imc," + lay_s + "->" + lay_i, residue * head_next, state_in, precision=HIGH
    )
    grad_gated = jnp.einsum("cij," + lay_i + "->" + lay_j, toeplitz, grad_b, precision=HIGH)
    grad_gated = grad_gated + jnp.einsum(
        "jmc," + lay_s + "->" + lay_j, residue * back, back_in, precision=HIGH
    )
    outer = jnp.einsum(lay_i + "," + lay_j + "->cij", grad_b, gated_b, precision=HIGH)
    correl = jnp.einsum("cij,ijk->kc", outer, onehot, precision=HIGH)
    near_w = jnp.einsum(lay_i + ",imc->" + lay_s, grad_b, head_next, precision=HIGH)
    near_t = jnp.einsum(lay_i + ",imc->" + lay_s, grad_b, (pos + 1.0) * head_next, precision=HIGH)
    pair = lay_s + "," + lay_s + "->mc"
    grad_residue = jnp.einsum("kc,kmc->mc", correl, head, precision=HIGH)
    grad_residue = grad_residue + jnp.einsum(pair, near_w, state_in, precision=HIGH)
    weighted = jnp.einsum("kc,kmc->mc", correl, pos * head, precision=HIGH)
    weighted = weighted + jnp.einsum(pair, near_t, state_in, precision=HIGH)
    weighted = weighted + jnp.einsum(pair, near_w, moment_in, precision=HIGH)
    grad_rate = -residue / seq_len * weighted
    scale = seq_len ** (-0.5)
    chans = conv.shape[0]
    rows = conv.shape[1] * BLK
    shape_out = (chans, rows)
    return (
        conv.reshape(shape_out).astype(jnp.bfloat16),
        grad_gated.reshape(shape_out).astype(jnp.bfloat16),
        scale * grad_residue,
        scale * grad_rate,
    )


def local(query, key_in, value, grad_out, residue, rate):
    gated = (key_in.astype(jnp.float32) * value.astype(jnp.float32)).astype(jnp.bfloat16)
    grad_conv = (grad_out.astype(jnp.float32) * query.astype(jnp.float32)).astype(jnp.bfloat16)
    gated_t = gated.T
    grad_t = grad_conv.T
    gated_ch, grad_ch = (
        lax.all_to_all(gated_t, "ctx", split_axis=0, concat_axis=1, tiled=True),
        lax.all_to_all(grad_t, "ctx", split_axis=0, concat_axis=1, tiled=True),
    )
    chans = gated_ch.shape[0]
    seq_len = gated_ch.shape[1]
    start = lax.axis_index("ctx") * chans
    residue_ch = lax.dynamic_slice_in_dim(residue, start, chans, 1)
    rate_ch = lax.dynamic_slice_in_dim(rate, start, chans, 1)
    tables, gated_b, grad_b, fwd_incl, rev_incl = prepare(gated_ch, grad_ch, rate_ch, seq_len)
    zero_span = jnp.zeros((1, 1, 1), jnp.float32)
    zero_state = jnp.zeros((1, 1, 1), jnp.float32)
    conv_ch, grad_gated_ch, own_res, own_rate = finish(
        tables,
        gated_b,
        grad_b,
        fwd_incl,
        rev_incl,
        (zero_span, zero_state, zero_state),
        (zero_span, zero_state),
        residue_ch,
        seq_len,
    )
    conv_t, grad_gated_t = (
        lax.all_to_all(conv_ch, "ctx", split_axis=1, concat_axis=0, tiled=True),
        lax.all_to_all(grad_gated_ch, "ctx", split_axis=1, concat_axis=0, tiled=True),
    )
    conv = conv_t.T
    grad_gated = grad_gated_t.T
    grad_residue, grad_rate = (
        lax.all_gather(own_res, "ctx", axis=1, tiled=True),
        lax.all_gather(own_rate, "ctx", axis=1, tiled=True),
    )
    conv_f = conv.astype(jnp.float32)
    grad_gated_f = grad_gated.astype(jnp.float32)
    grad_query = (grad_out.astype(jnp.float32) * conv_f).astype(jnp.bfloat16)
    grad_key = (grad_gated_f * value.astype(jnp.float32)).astype(jnp.bfloat16)
    grad_value = (grad_gated_f * key_in.astype(jnp.float32)).astype(jnp.bfloat16)
    return (grad_query, grad_key, grad_value, grad_residue, grad_rate)


def solution(mesh):
    in_specs = (
        P("ctx", "tp"),
        P("ctx", "tp"),
        P("ctx", "tp"),
        P("ctx", "tp"),
        P(None, "tp"),
        P(None, "tp"),
    )
    out_specs = (P("ctx", "tp"), P("ctx", "tp"), P("ctx", "tp"), P(None, "tp"), P(None, "tp"))
    return jax.shard_map(local, mesh=mesh, in_specs=in_specs, out_specs=out_specs, check_vma=False)
```

profile of v0, /device:TPU:1, one launch (start us, length us, event | category | flops | bytes accessed | tf_op | source)
XLA Modules:
  0.0 864.4 jit_solution(11036327460467527053)
XLA Ops:
  3.1 17.0 %all-to-all-start.2 = ((bf16[128,8,256]{2,1,0:T(8,128)(2,1)}), bf16[128,8,256]{2,1,0:T(8,128)(2,1)S(1)}, u32[]{:S(2)}, u32[]{:S(2)}) async-start(bf16[128,8,256]{2,1,0:T(8,128)(2,1)} %fusion.14), calls=%async_computation.2 | async-start | bytes 1048576 | tf_op jit(solution)/shard_map/all_to_all | solution.py:122
  21.5 6.5 fusion.1
  28.0 14.1 %all-to-all-done.2 = bf16[128,8,256]{2,1,0:T(8,128)(2,1)S(1)} async-done(((bf16[128,8,256]{2,1,0:T(8,128)(2,1)}), bf16[128,8,256]{2,1,0:T(8,128)(2,1)S(1)}, u32[]{:S(2)}, u32[]{:S(2)}) %all-to-all-start.2) | async-done | bytes 524320 | tf_op jit(solution)/shard_map/all_to_all | solution.py:122
  53.7 44.0 %pad.368 = f32[8,16,256]{1,0,2:T(8,128)S(1)} pad(f32[8,16,128]{1,0,2:T(8,128)} %add.470, f32[]{:T(128)} %constant.112.clone.1), padding=0_0_0x0_0_0x1_0_1 | pad | bytes 196612
  102.6 44.0 %pad.279 = f32[8,16,255]{1,0,2:T(8,128)S(1)} pad(f32[8,16,128]{1,0,2:T(8,128)} %pad_maximum_fusion.1, f32[]{:T(128)} %constant.112.clone.1), padding=0_0_0x0_0_0x0_0_1 | pad | bytes 196100 | tf_op jit(solution)/shard_map/slice | solution.py:70
  152.5 5.8 all-to-all-start.3
  159.5 20.9 %all-to-all-done.3 = bf16[8,128,256]{2,0,1:T(8,128)(2,1)S(1)} async-done(((bf16[8,128,256]{2,0,1:T(8,128)(2,1)}), bf16[8,128,256]{2,0,1:T(8,128)(2,1)S(1)}, u32[]{:S(2)}, u32[]{:S(2)}) %all-to-all-start.3) | async-done | bytes 524320 | tf_op jit(solution)/shard_map/all_to_all | solution.py:145
  182.6 5.5 all-to-all-start
  193.9 16.3 %all-to-all-done = bf16[128,8,256]{2,1,0:T(8,128)(2,1)S(1)} async-done(((bf16[128,8,256]{2,1,0:T(8,128)(2,1)}), bf16[128,8,256]{2,1,0:T(8,128)(2,1)S(1)}, u32[]{:S(2)}, u32[]{:S(2)}) %all-to-all-start) | async-done | bytes 524320 | tf_op jit(solution)/shard_map/all_to_all | solution.py:121
  266.4 4.6 pad.190
  270.9 4.5 pad.191
  275.5 4.6 pad.223
  281.4 4.5 pad.222
  291.9 5.5 pad.193
  298.8 8.3 pad.224
  307.1 8.3 pad.225
  320.1 10.9 %pad.227 = f32[8,16,64]{1,0,2:T(8,128)S(1)} pad(f32[8,16,32]{1,0,2:T(8,128)} %add.505, f32[]{:T(128)} %constant.112.clone.1), padding=0_0_0x0_0_0x1_0_1 | pad | bytes 49156 | tf_op jit(solution)/shard_map/pad | solution.py:51
  332.5 15.0 %pad.226 = f32[8,16,64]{1,0,2:T(8,128)} pad(f32[8,16,32]{1,0,2:T(8,128)} %pad_maximum_fusion.8, f32[]{:T(128)} %constant.112.clone.1), padding=0_0_0x0_0_0x0_1_1 | pad | bytes 49156 | tf_op jit(solution)/shard_map/pad | solution.py:51
  361.3 38.7 %pad.369 = f32[8,16,256]{1,0,2:T(8,128)} pad(f32[8,16,128]{1,0,2:T(8,128)S(1)} %add.511, f32[]{:T(128)} %constant.112.clone.1), padding=0_0_0x0_0_0x1_0_1 | pad | bytes 196612
  405.1 38.7 %pad.281 = f32[8,16,255]{1,0,2:T(8,128)} pad(f32[8,16,128]{1,0,2:T(8,128)S(1)} %pad_maximum_fusion.2, f32[]{:T(128)} %constant.112.clone.1), padding=0_0_0x0_0_0x0_0_1 | pad | bytes 196100 | tf_op jit(solution)/shard_map/slice | solution.py:64
  445.0 38.7 %pad.277 = f32[8,16,255]{1,0,2:T(8,128)} pad(f32[8,16,128]{1,0,2:T(8,128)S(1)} %pad_maximum_fusion, f32[]{:T(128)} %constant.112.clone.1), padding=0_0_0x0_0_0x0_0_1 | pad | bytes 196100 | tf_op jit(solution)/shard_map/slice | solution.py:64
  491.5 5.7 all-to-all-start.1
  499.8 184.7 %all_gather.7 = f32[16,1024]{0,1:T(8,128)S(1)} all-gather(f32[16,8]{0,1:T(8,128)S(1)} %multiply_multiply_fusion), channel_id=1, replica_groups=mesh['ctx'=128,'tp'=2] {'ctx'}, dimensions={1}, use_global_device_ids=true | all-gather | bytes 66048 | tf_op jit(solution)/shard_map/all_gather | solution.py:151
  685.6 176.6 %all_gather.6 = f32[16,1024]{0,1:T(8,128)S(1)} all-gather(f32[16,8]{0,1:T(8,128)S(1)} %add_multiply_fusion.6), channel_id=1, replica_groups=mesh['ctx'=128,'tp'=2] {'ctx'}, dimensions={1}, use_global_device_ids=true | all-gather | bytes 66048 | tf_op jit(solution)/shard_map/all_gather | solution.py:150
  (300 shorter events, 138.9 us)
Async XLA Ops:
  3.1 39.0 %all-to-all-start.2 = ((bf16[128,8,256]{2,1,0:T(8,128)(2,1)}), bf16[128,8,256]{2,1,0:T(8,128)(2,1)S(1)}, u32[]{:S(2)}, u32[]{:S(2)}) async-start(bf16[128,8,256]{2,1,0:T(8,128)(2,1)} %fusion.14), calls=%async_computation.2 | async-start | bytes 1048576 | tf_op jit(solution)/shard_map/all_to_all | solution.py:122
  21.1 129.0 %copy-start.39 = (f32[16,8]{0,1:T(8,128)}, f32[16,8]{0,1:T(8,128)S(1)}, u32[]{:S(2)}) copy-start(f32[16,8]{0,1:T(8,128)S(1)} %copy.254) | copy-start | bytes 1540
  21.1 6.9 copy-start.41
  21.1 128.5 %copy-start.37 = (f32[8,16]{1,0:T(8,128)}, f32[8,16]{1,0:T(8,128)S(1)}, u32[]{:S(2)}) copy-start(f32[8,16]{1,0:T(8,128)S(1)} %get-tuple-element.84) | copy-start | bytes 1540
  21.4 26.6 %copy-start.43 = (f32[8,16]{1,0:T(8,128)}, f32[8,16]{1,0:T(8,128)S(1)}, u32[]{:S(2)}) copy-start(f32[8,16]{1,0:T(8,128)S(1)} %get-tuple-element.86) | copy-start | bytes 1540
  21.4 26.8 %copy-start.35 = (f32[8,16]{1,0:T(8,128)}, f32[8,16]{1,0:T(8,128)S(1)}, u32[]{:S(2)}) copy-start(f32[8,16]{1,0:T(8,128)S(1)} %get-tuple-element.87) | copy-start | bytes 1540
  21.4 26.9 %copy-start.33 = (f32[8,16]{1,0:T(8,128)}, f32[8,16]{1,0:T(8,128)S(1)}, u32[]{:S(2)}) copy-start(f32[8,16]{1,0:T(8,128)S(1)} %get-tuple-element.88) | copy-start | bytes 1540
  21.4 27.1 %copy-start.31 = (f32[8,16]{1,0:T(8,128)}, f32[8,16]{1,0:T(8,128)S(1)}, u32[]{:S(2)}) copy-start(f32[8,16]{1,0:T(8,128)S(1)} %get-tuple-element.89) | copy-start | bytes 1540
  21.5 27.4 %copy-start.28 = (f32[8,16]{1,0:T(8,128)}, f32[8,16]{1,0:T(8,128)S(1)}, u32[]{:S(2)}) copy-start(f32[8,16]{1,0:T(8,128)S(1)} %get-tuple-element.90) | copy-start | bytes 1540
  151.4 6.9 copy-start.22
  152.5 6.0 copy-start.23
  152.5 27.9 %all-to-all-start.3 = ((bf16[8,128,256]{2,0,1:T(8,128)(2,1)}), bf16[8,128,256]{2,0,1:T(8,128)(2,1)S(1)}, u32[]{:S(2)}, u32[]{:S(2)}) async-start(bf16[8,128,256]{2,0,1:T(8,128)(2,1)} %copy.217), calls=%async_computation.3 | async-start | bytes 1048576 | tf_op jit(solution)/shard_map/all_to_all | solution.py:145
  182.6 27.6 %all-to-all-start = ((bf16[128,8,256]{2,1,0:T(8,128)(2,1)}), bf16[128,8,256]{2,1,0:T(8,128)(2,1)S(1)}, u32[]{:S(2)}, u32[]{:S(2)}) async-start(bf16[128,8,256]{2,1,0:T(8,128)(2,1)} %get-tuple-element.53), calls=%async_computation | async-start | bytes 1048576 | tf_op jit(solution)/shard_map/all_to_all | solution.py:121
  211.1 146.0 %copy-start.11 = (f32[8,16,256]{2,1,0:T(8,128)}, f32[8,16,256]{2,1,0:T(8,128)S(1)}, u32[]{:S(2)}) copy-start(f32[8,16,256]{2,1,0:T(8,128)S(1)} %fusion.39) | copy-start | bytes 393220
  216.1 6.7 copy-start.12
  287.4 28.6 %copy-start.30 = (f32[8,16]{1,0:T(8,128)S(1)}, f32[8,16]{1,0:T(8,128)}, u32[]{:S(2)}) copy-start(f32[8,16]{1,0:T(8,128)} %copy-done.28) | copy-start | bytes 1540
  315.4 4.2 copy-start.46
  351.7 6.5 copy-start.8
  361.3 38.7 %copy-start.17 = (f32[8,16,63]{1,0,2:T(8,128)S(1)}, f32[8,16,63]{1,0,2:T(8,128)}, u32[]{:S(2)}) copy-start(f32[8,16,63]{1,0,2:T(8,128)} %get-tuple-element.46) | copy-start | bytes 96772
  405.1 38.8 %copy-start.6 = (f32[8,16,128]{1,0,2:T(8,128)S(1)}, f32[8,16,128]{1,0,2:T(8,128)}, u32[]{:S(2)}) copy-start(f32[8,16,128]{1,0,2:T(8,128)} %add.444) | copy-start | bytes 196612
  444.9 38.8 %copy-start.19 = (f32[8,128,128]{2,1,0:T(8,128)S(1)}, f32[8,128,128]{2,1,0:T(8,128)}, u32[]{:S(2)}) copy-start(f32[8,128,128]{2,1,0:T(8,128)} %fusion.83) | copy-start | bytes 1572868
  444.9 38.8 %copy-start.42 = (s32[128,128]{1,0:T(8,128)S(1)}, s32[128,128]{1,0:T(8,128)}, u32[]{:S(2)}) copy-start(s32[128,128]{1,0:T(8,128)} %copy-done.41) | copy-start | bytes 196612
  490.4 6.8 copy-start.3
  491.5 371.5 %all-to-all-start.1 = ((bf16[8,128,256]{2,0,1:T(8,128)(2,1)}), bf16[8,128,256]{2,0,1:T(8,128)(2,1)S(1)}, u32[]{:S(2)}, u32[]{:S(2)}) async-start(bf16[8,128,256]{2,0,1:T(8,128)(2,1)} %copy.208), calls=%async_computation.1 | async-start | bytes 1048576 | tf_op jit(solution)/shard_map/all_to_all | solution.py:144
  (34 other events, 51.2 us)
where the time goes:
time: 876 us; the launch traced here: 864 us
  blocking collectives  361 us (41%)
  local copies, waits for them, and re-layouts  348 us (40%)
  waiting for transfers between devices  51.4 us (6%)
  other arithmetic  48.1 us (5%)
  starting transfers between devices  34 us (4%)
  matrix products  19.2 us (2%)
    all_gather x1, blocking collectives, local(): lax.all_gather(own_rate, 'ctx', axis=1, tiled=True)  185 us
    all_gather x1, blocking collectives, local(): lax.all_gather(own_res, 'ctx', axis=1, tiled=True)  177 us
    unnamed x130, local copies, waits for them, and re-layouts  104 us
    pad x24, local copies, waits for them, and re-layouts, prepare(): lax.associative_scan(partial(combine_fwd, lam_s), (spans, state_sum, mome...  88.6 us
    slice x2, local copies, waits for them, and re-layouts, shift_down(): lax.slice_in_dim(arr, 0, count - 1, axis=axis_b)  77.4 us
    slice x2, local copies, waits for them, and re-layouts, shift_up(): lax.slice_in_dim(arr, 1, count, axis=axis_b)  45.3 us
    all_to_all x1, waiting for transfers between devices, local(): lax.all_to_all(grad_gated_ch, 'ctx', split_axis=1, concat_axis=0, tiled=T...  20.9 us
    slice x20, local copies, waits for them, and re-layouts, prepare(): lax.associative_scan(partial(combine_fwd, lam_s), (spans, state_sum, mome...  20.2 us
  transfers between devices with their start and end apart: 4, of which 3 were waited for; matrix products, arithmetic and copies ran while one was open for 2% of the time, Pallas kernels for 0%

commit v1 on v0

--- a/solution.py
+++ b/solution.py
@@ -6,6 +6,11 @@
 
 BLK = 128
 HIGH = lax.Precision.HIGHEST
+
+
+def gather_over(value, mesh_axis, d):
+    outgoing = jnp.stack([value] * lax.axis_size(mesh_axis))
+    return jnp.concatenate(lax.all_to_all(outgoing, mesh_axis, 0, 0), axis=d)
 
 
 def combine_fwd(lam, earlier, later):
@@ -147,7 +152,7 @@
     conv = conv_t.T
     grad_gated = grad_gated_t.T
     grad_residue, grad_rate = (
-        lax.all_gather(own_res, "ctx", axis=1, tiled=True),
+        gather_over(own_res, "ctx", 1),
         lax.all_gather(own_rate, "ctx", axis=1, tiled=True),
     )
     conv_f = conv.astype(jnp.float32)

time: 876 us -> 684 us (0.78)
  blocking collectives: 361 us -> 185 us
  local copies, waits for them, and re-layouts: 348 us -> 314 us
  waiting for transfers between devices: 51.4 us -> 64 us
    all_gather x1 -> x0, blocking collectives: 177 us -> none  [local(): lax.all_gather(own_res, 'ctx', axis=1, tiled=True)]
    slice x2, local copies, waits for them, and re-layouts: 77.4 us -> 39.7 us  [shift_down(): lax.slice_in_dim(arr, 0, count - 1, axis=axis_b)]
    all_to_all x0 -> x1, waiting for transfers between devices: none -> 9.87 us  [gather_over(): return jnp.concatenate(lax.all_to_all(outgoing, mesh_axis, 0, 0), axis=d)]
    unnamed x130 -> x131, local copies, waits for them, and re-layouts: 104 us -> 107 us
  transfers between devices with their start and end apart: 4 -> 5, of which waited for: 3 -> 4; matrix products, arithmetic and copies ran while one was open for 2% -> 3% of each run, Pallas kernels for 0% -> 0%
where the time goes in v1:
time: 684 us; the launch traced here: 672 us
  local copies, waits for them, and re-layouts  314 us (46%)
  blocking collectives  185 us (27%)
  waiting for transfers between devices  64 us (9%)
  other arithmetic  46.5 us (7%)
  starting transfers between devices  39.8 us (6%)
  matrix products  20.4 us (3%)
    all_gather x1, blocking collectives, local(): lax.all_gather(own_rate, 'ctx', axis=1, tiled=True)  185 us
    unnamed x131, local copies, waits for them, and re-layouts  107 us
    pad x24, local copies, waits for them, and re-layouts, prepare(): lax.associative_scan(partial(combine_fwd, lam_s), (spans, state_sum, mome...  88.5 us
    slice x2, local copies, waits for them, and re-layouts, shift_up(): lax.slice_in_dim(arr, 1, count, axis=axis_b)  45.3 us
    slice x2, local copies, waits for them, and re-layouts, shift_down(): lax.slice_in_dim(arr, 0, count - 1, axis=axis_b)  39.7 us
    all_to_all x1, waiting for transfers between devices, local(): lax.all_to_all(grad_gated_ch, 'ctx', split_axis=1, concat_axis=0, tiled=T...  21.7 us
    slice x20, local copies, waits for them, and re-layouts, prepare(): lax.associative_scan(partial(combine_fwd, lam_s), (spans, state_sum, mome...  20.3 us
    all_to_all x1, waiting for transfers between devices, local(): lax.all_to_all(gated_t, 'ctx', split_axis=0, concat_axis=1, tiled=True)  18.3 us
  transfers between devices with their start and end apart: 5, of which 4 were waited for; matrix products, arithmetic and copies ran while one was open for 3% of the time, Pallas kernels for 0%

profile of v1, /device:TPU:1, one launch (start us, length us, event | category | flops | bytes accessed | tf_op | source)
XLA Modules:
  0.0 671.7 jit_solution(9820914066035875867)
XLA Ops:
  3.1 17.0 %all-to-all-start.2 = ((bf16[128,8,256]{2,1,0:T(8,128)(2,1)}), bf16[128,8,256]{2,1,0:T(8,128)(2,1)S(1)}, u32[]{:S(2)}, u32[]{:S(2)}) async-start(bf16[128,8,256]{2,1,0:T(8,128)(2,1)} %fusion.14), calls=%async_computation.2 | async-start | bytes 1048576 | tf_op jit(solution)/shard_map/all_to_all | solution.py:127
  21.5 6.5 fusion.1
  28.0 14.1 %all-to-all-done.2 = bf16[128,8,256]{2,1,0:T(8,128)(2,1)S(1)} async-done(((bf16[128,8,256]{2,1,0:T(8,128)(2,1)}), bf16[128,8,256]{2,1,0:T(8,128)(2,1)S(1)}, u32[]{:S(2)}, u32[]{:S(2)}) %all-to-all-start.2) | async-done | bytes 524320 | tf_op jit(solution)/shard_map/all_to_all | solution.py:127
  53.7 44.0 %pad.368 = f32[8,16,256]{1,0,2:T(8,128)S(1)} pad(f32[8,16,128]{1,0,2:T(8,128)} %add.470, f32[]{:T(128)} %constant.112.clone.1), padding=0_0_0x0_0_0x1_0_1 | pad | bytes 196612
  102.6 44.0 %pad.279 = f32[8,16,255]{1,0,2:T(8,128)S(1)} pad(f32[8,16,128]{1,0,2:T(8,128)} %pad_maximum_fusion.1, f32[]{:T(128)} %constant.112.clone.1), padding=0_0_0x0_0_0x0_0_1 | pad | bytes 196100 | tf_op jit(solution)/shard_map/slice | solution.py:75
  152.5 5.8 all-to-all-start.3
  158.7 21.7 %all-to-all-done.3 = bf16[8,128,256]{2,0,1:T(8,128)(2,1)S(1)} async-done(((bf16[8,128,256]{2,0,1:T(8,128)(2,1)}), bf16[8,128,256]{2,0,1:T(8,128)(2,1)S(1)}, u32[]{:S(2)}, u32[]{:S(2)}) %all-to-all-start.3) | async-done | bytes 524320 | tf_op jit(solution)/shard_map/all_to_all | solution.py:150
  182.1 5.4 all-to-all-start
  191.4 18.3 %all-to-all-done = bf16[128,8,256]{2,1,0:T(8,128)(2,1)S(1)} async-done(((bf16[128,8,256]{2,1,0:T(8,128)(2,1)}), bf16[128,8,256]{2,1,0:T(8,128)(2,1)S(1)}, u32[]{:S(2)}, u32[]{:S(2)}) %all-to-all-start) | async-done | bytes 524320 | tf_op jit(solution)/shard_map/all_to_all | solution.py:126
  265.8 4.6 pad.190
  274.9 4.5 pad.223
  280.8 4.5 pad.222
  291.4 5.4 pad.193
  298.3 8.3 %pad.224 = f32[8,16,32]{1,0,2:T(8,128)} pad(f32[8,16,16]{1,0,2:T(8,128)} %pad_maximum_fusion.11, f32[]{:T(128)} %constant.112.clone.1), padding=0_0_0x0_0_0x0_1_1 | pad | bytes 24580 | tf_op jit(solution)/shard_map/pad | solution.py:56
  306.6 8.3 %pad.225 = f32[8,16,32]{1,0,2:T(8,128)} pad(f32[8,16,16]{1,0,2:T(8,128)} %add.502, f32[]{:T(128)} %constant.112.clone.1), padding=0_0_0x0_0_0x1_0_1 | pad | bytes 24580 | tf_op jit(solution)/shard_map/pad | solution.py:56
  319.6 10.9 %pad.227 = f32[8,16,64]{1,0,2:T(8,128)S(1)} pad(f32[8,16,32]{1,0,2:T(8,128)} %add.505, f32[]{:T(128)} %constant.112.clone.1), padding=0_0_0x0_0_0x1_0_1 | pad | bytes 49156 | tf_op jit(solution)/shard_map/pad | solution.py:56
  332.0 14.9 %pad.226 = f32[8,16,64]{1,0,2:T(8,128)} pad(f32[8,16,32]{1,0,2:T(8,128)} %pad_maximum_fusion.8, f32[]{:T(128)} %constant.112.clone.1), padding=0_0_0x0_0_0x0_1_1 | pad | bytes 49156 | tf_op jit(solution)/shard_map/pad | solution.py:56
  360.1 38.7 %pad.369 = f32[8,16,256]{1,0,2:T(8,128)} pad(f32[8,16,128]{1,0,2:T(8,128)S(1)} %add.511, f32[]{:T(128)} %constant.112.clone.1), padding=0_0_0x0_0_0x1_0_1 | pad | bytes 196612
  407.4 38.7 %pad.277 = f32[8,16,255]{1,0,2:T(8,128)} pad(f32[8,16,128]{1,0,2:T(8,128)S(1)} %pad_maximum_fusion, f32[]{:T(128)} %constant.112.clone.1), padding=0_0_0x0_0_0x0_0_1 | pad | bytes 196100 | tf_op jit(solution)/shard_map/slice | solution.py:69
  446.1 4.5 fusion
  456.0 5.7 all-to-all-start.4
  464.2 9.9 %all-to-all-done.4 = f32[128,1,128]{2,1,0:T(1,128)S(1)} async-done(((f32[128,1,128]{2,1,0:T(1,128)}), f32[128,1,128]{2,1,0:T(1,128)S(1)}, u32[]{:S(2)}, u32[]{:S(2)}) %all-to-all-start.4) | async-done | bytes 65568 | tf_op jit(solution)/shard_map/all_to_all | solution.py:13
  474.1 5.8 all-to-all-start.1
  482.3 184.7 %all_gather.3 = f32[16,1024]{0,1:T(8,128)S(1)} all-gather(f32[16,8]{0,1:T(8,128)S(1)} %multiply_multiply_fusion), channel_id=1, replica_groups=mesh['ctx'=128,'tp'=2] {'ctx'}, dimensions={1}, use_global_device_ids=true | all-gather | bytes 66048 | tf_op jit(solution)/shard_map/all_gather | solution.py:156
  (305 shorter events, 142.9 us)
Async XLA Ops:
  3.1 39.0 %all-to-all-start.2 = ((bf16[128,8,256]{2,1,0:T(8,128)(2,1)}), bf16[128,8,256]{2,1,0:T(8,128)(2,1)S(1)}, u32[]{:S(2)}, u32[]{:S(2)}) async-start(bf16[128,8,256]{2,1,0:T(8,128)(2,1)} %fusion.14), calls=%async_computation.2 | async-start | bytes 1048576 | tf_op jit(solution)/shard_map/all_to_all | solution.py:127
  21.1 129.0 %copy-start.38 = (f32[16,8]{0,1:T(8,128)}, f32[16,8]{0,1:T(8,128)S(1)}, u32[]{:S(2)}) copy-start(f32[16,8]{0,1:T(8,128)S(1)} %copy.254) | copy-start | bytes 1540
  21.1 6.9 %copy-start.40 = (s32[128,128]{1,0:T(8,128)}, s32[128,128]{1,0:T(8,128)S(1)}, u32[]{:S(2)}) copy-start(s32[128,128]{1,0:T(8,128)S(1)} %iota_subtract_fusion) | copy-start | bytes 196612
  21.1 128.5 %copy-start.36 = (f32[8,16]{1,0:T(8,128)}, f32[8,16]{1,0:T(8,128)S(1)}, u32[]{:S(2)}) copy-start(f32[8,16]{1,0:T(8,128)S(1)} %get-tuple-element.84) | copy-start | bytes 1540
  21.4 26.6 %copy-start.42 = (f32[8,16]{1,0:T(8,128)}, f32[8,16]{1,0:T(8,128)S(1)}, u32[]{:S(2)}) copy-start(f32[8,16]{1,0:T(8,128)S(1)} %get-tuple-element.86) | copy-start | bytes 1540
  21.4 26.7 %copy-start.34 = (f32[8,16]{1,0:T(8,128)}, f32[8,16]{1,0:T(8,128)S(1)}, u32[]{:S(2)}) copy-start(f32[8,16]{1,0:T(8,128)S(1)} %get-tuple-element.87) | copy-start | bytes 1540
  21.4 26.9 %copy-start.32 = (f32[8,16]{1,0:T(8,128)}, f32[8,16]{1,0:T(8,128)S(1)}, u32[]{:S(2)}) copy-start(f32[8,16]{1,0:T(8,128)S(1)} %get-tuple-element.88) | copy-start | bytes 1540
  21.4 27.1 %copy-start.30 = (f32[8,16]{1,0:T(8,128)}, f32[8,16]{1,0:T(8,128)S(1)}, u32[]{:S(2)}) copy-start(f32[8,16]{1,0:T(8,128)S(1)} %get-tuple-element.89) | copy-start | bytes 1540
  21.5 27.4 %copy-start.27 = (f32[8,16]{1,0:T(8,128)}, f32[8,16]{1,0:T(8,128)S(1)}, u32[]{:S(2)}) copy-start(f32[8,16]{1,0:T(8,128)S(1)} %get-tuple-element.90) | copy-start | bytes 1540
  151.4 6.9 %copy-start.21 = (bf16[256,1024]{1,0:T(8,128)(2,1)S(1)}, bf16[256,1024]{1,0:T(8,128)(2,1)}, u32[]{:S(2)}) copy-start(bf16[256,1024]{1,0:T(8,128)(2,1)} %param.7) | copy-start | bytes 1572868
  152.5 27.9 %all-to-all-start.3 = ((bf16[8,128,256]{2,0,1:T(8,128)(2,1)}), bf16[8,128,256]{2,0,1:T(8,128)(2,1)S(1)}, u32[]{:S(2)}, u32[]{:S(2)}) async-start(bf16[8,128,256]{2,0,1:T(8,128)(2,1)} %copy.217), calls=%async_computation.3 | async-start | bytes 1048576 | tf_op jit(solution)/shard_map/all_to_all | solution.py:150
  182.1 27.6 %all-to-all-start = ((bf16[128,8,256]{2,1,0:T(8,128)(2,1)}), bf16[128,8,256]{2,1,0:T(8,128)(2,1)S(1)}, u32[]{:S(2)}, u32[]{:S(2)}) async-start(bf16[128,8,256]{2,1,0:T(8,128)(2,1)} %get-tuple-element.53), calls=%async_computation | async-start | bytes 1048576 | tf_op jit(solution)/shard_map/all_to_all | solution.py:126
  210.6 145.2 %copy-start.12 = (f32[8,16,256]{2,1,0:T(8,128)}, f32[8,16,256]{2,1,0:T(8,128)S(1)}, u32[]{:S(2)}) copy-start(f32[8,16,256]{2,1,0:T(8,128)S(1)} %fusion.39) | copy-start | bytes 393220
  215.6 6.7 copy-start.13
  286.9 28.6 %copy-start.29 = (f32[8,16]{1,0:T(8,128)S(1)}, f32[8,16]{1,0:T(8,128)}, u32[]{:S(2)}) copy-start(f32[8,16]{1,0:T(8,128)} %copy-done.27) | copy-start | bytes 1540
  360.1 38.7 %copy-start.17 = (f32[8,16,63]{1,0,2:T(8,128)S(1)}, f32[8,16,63]{1,0,2:T(8,128)}, u32[]{:S(2)}) copy-start(f32[8,16,63]{1,0,2:T(8,128)} %get-tuple-element.46) | copy-start | bytes 96772
  406.2 39.8 %copy-start.41 = (s32[128,128]{1,0:T(8,128)S(1)}, s32[128,128]{1,0:T(8,128)}, u32[]{:S(2)}) copy-start(s32[128,128]{1,0:T(8,128)} %copy-done.40) | copy-start | bytes 196612
  455.1 6.6 copy-start.2
  455.1 6.6 copy-start.39
  455.1 6.6 copy-start.47
  456.0 18.1 %all-to-all-start.4 = ((f32[128,1,128]{2,1,0:T(1,128)}), f32[128,1,128]{2,1,0:T(1,128)S(1)}, u32[]{:S(2)}, u32[]{:S(2)}) async-start(f32[128,1,128]{2,1,0:T(1,128)} %reshape.115), calls=%async_computation.4 | async-start | bytes 131072 | tf_op jit(solution)/shard_map/all_to_all | solution.py:13
  463.1 16.8 %copy-start.7 = (bf16[256,1024]{0,1:T(8,128)(2,1)S(1)}, bf16[256,1024]{0,1:T(8,128)(2,1)}, u32[]{:S(2)}) copy-start(bf16[256,1024]{0,1:T(8,128)(2,1)} %get-tuple-element.52) | copy-start | bytes 1572868
  464.2 16.7 %copy-start.6 = (bf16[256,1024]{0,1:T(8,128)(2,1)S(1)}, bf16[256,1024]{0,1:T(8,128)(2,1)}, u32[]{:S(2)}) copy-start(bf16[256,1024]{0,1:T(8,128)(2,1)} %get-tuple-element.51) | copy-start | bytes 1572868
  474.1 196.1 %all-to-all-start.1 = ((bf16[8,128,256]{2,0,1:T(8,128)(2,1)}), bf16[8,128,256]{2,0,1:T(8,128)(2,1)S(1)}, u32[]{:S(2)}, u32[]{:S(2)}) async-start(bf16[8,128,256]{2,0,1:T(8,128)(2,1)} %copy.208), calls=%async_computation.1 | async-start | bytes 1048576 | tf_op jit(solution)/shard_map/all_to_all | solution.py:149
  (34 other events, 65.6 us)
